TPU v7x, 512 devices: a whole 4x4x16 slice. The times are simulated.
512 devices in a mesh: grp: 16 (over y, x), wide: 32 (over z, core).
Axes of the slice: x: 4, y: 4, z: 16, core: 2. Of those that a mesh axis runs over, the one named last changes fastest.
Arguments:
- null_space: bfloat16 [16, 4096, 1152], P('grp', 'wide'), may hold values from -6 to 6
- node_damage: int32 [16, 4096, 64], P('grp', 'wide'), may hold values from 0 to 7
- face_target: int32 [16, 4096, 3], P('grp', 'wide'), may hold values from 0 to 191
- face_damage: int32 [16, 4096, 3], P('grp', 'wide'), may hold values from 0 to 7
- ghost_lists: int32 [16, 32, 4, 16], P('grp', 'wide'), may hold values from 0 to 127
- agg_owner: int32 [16, 4096, 1], P('grp', 'wide'), may hold values from 0 to 31; in each aligned block of 128 rows (0 to 127, 128 to 255, ..., all dimensions but the last counted through in order) at most 8 rows name the same one
- stiffness: bfloat16 [192, 768], replicated, as said below
Outputs:
- coarse_rows: float32 [16, 4608, 256], P('grp', 'wide')
Inputs may be any that keep to these rules, and one draw needn't show every extreme that they name: `agg_owner`: no more than 8 aggregates of one device share an owner, and exactly that many do on some device. `stiffness`: each 192 x 192 block is symmetric.
All inputs are finite; a program needn't handle non-finite values.
Results may differ from a plain program's by a relative error of at most 0.0027.
Values may be sent and summed in bfloat16 or wider, within the bound.
A program may use at most 64 MiB of HBM per device.

v0:
```python
import jax
import jax.numpy as jnp
from jax import lax
from jax.sharding import PartitionSpec as P

MODES = 6
LEVELS = 8


def padded(block, sides, width):
    for axis, dim in sides:
        count = lax.axis_size(axis)
        forward = [(i, i + 1) for i in range(count - 1)]
        backward = [(target, source) for source, target in forward]
        low = lax.ppermute(
            lax.slice_in_dim(block, block.shape[dim] - width, None, axis=dim), axis, forward
        )
        high = lax.ppermute(lax.slice_in_dim(block, 0, width, axis=dim), axis, backward)
        block = jnp.concatenate([low, block, high], axis=dim)
    return block


def project(left, matrix):
    count, modes_count, dofs_count = left.shape
    product = jnp.dot(
        left.reshape(count * modes_count, dofs_count), matrix, preferred_element_type=jnp.float32
    )
    return product.astype(jnp.bfloat16).reshape(count, modes_count, dofs_count)


def paired(left, right):
    return jnp.einsum("amd,and->amn", left, right, preferred_element_type=jnp.float32)


def shards(null_space, node_damage, face_target, face_damage, ghost_lists, agg_owner, stiffness):
    agg_count = null_space.shape[1]
    modes_count = MODES
    dofs_count = null_space.shape[2] // modes_count
    face_count = face_target.shape[2]
    ghost_count = ghost_lists.shape[3]
    block_size = modes_count * modes_count
    row_size = (1 + face_count) * block_size
    wide_size = lax.axis_size("wide")
    send_cap = 2 * agg_count // wide_size
    interior_stiff = stiffness[:, :dofs_count]
    scales = (LEVELS - node_damage[0]).astype(jnp.float32) / LEVELS
    scales = jnp.repeat(scales, 3, axis=-1)
    raw_modes = null_space[0].reshape(agg_count, modes_count, dofs_count)
    modes = (raw_modes.astype(jnp.float32) * scales[:, None, :]).astype(jnp.bfloat16)
    listed = ghost_lists[0, 0]
    picked = modes[listed]
    grp_padded = padded(jnp.stack([picked[0], picked[1]]), (("grp", 0),), 1)
    wide_padded = padded(jnp.stack([picked[2], picked[3]]), (("wide", 0),), 1)
    diag = paired(project(modes, interior_stiff), modes)
    nears = []
    weights = []
    face_mats = []
    for index in range(face_count):
        face_matrix = stiffness[:, (index + 1) * dofs_count : (index + 2) * dofs_count]
        level = (LEVELS - face_damage[0, :, index]).astype(jnp.float32) / LEVELS
        weight = (level * level)[:, None, None]
        near = project(modes, face_matrix)
        diag = diag + weight * paired(near, modes)
        nears.append(near)
        weights.append(weight)
        face_mats.append(face_matrix)
    lookup = jnp.concatenate(
        [modes, grp_padded[0], grp_padded[3], wide_padded[0], wide_padded[3]], axis=0
    )
    face_blocks = []
    contribs = []
    for index in range(face_count):
        other = lookup[face_target[0, :, index]]
        far = project(other, face_mats[index])
        face_blocks.append(-weights[index] * paired(nears[index], other))
        contribs.append(weights[index] * paired(far, other))
    span = agg_count + 4 * ghost_count
    all_targets = jnp.transpose(face_target[0]).reshape(-1)
    selector = (all_targets[:, None] == jnp.arange(span, dtype=jnp.int32)[None, :]).astype(
        jnp.float32
    )
    values = jnp.stack(contribs).reshape(face_count * agg_count, block_size)
    buckets = jnp.einsum("ft,fc->tc", selector, values, precision=lax.Precision.HIGHEST)
    returns = buckets[agg_count:].reshape(4, ghost_count, block_size)
    back_grp = padded(jnp.stack([returns[0], returns[1]]), (("grp", 0),), 1)
    back_wide = padded(jnp.stack([returns[2], returns[3]]), (("wide", 0),), 1)
    incoming = jnp.stack([back_grp[0], back_grp[3], back_wide[0], back_wide[3]]).reshape(
        4 * ghost_count, block_size
    )
    list_select = (
        listed.reshape(-1)[:, None] == jnp.arange(agg_count, dtype=jnp.int32)[None, :]
    ).astype(jnp.float32)
    added = jnp.einsum("ga,gc->ac", list_select, incoming, precision=lax.Precision.HIGHEST)
    diag_total = diag.reshape(agg_count, block_size) + buckets[:agg_count] + added
    faces = jnp.stack(face_blocks, axis=1).reshape(agg_count, face_count * block_size)
    coarse = jnp.concatenate([diag_total, faces], axis=-1)
    owners = agg_owner[0, :, 0]
    onehot = (owners[:, None] == jnp.arange(wide_size, dtype=jnp.int32)[None, :]).astype(jnp.int32)
    ranks = jnp.sum((jnp.cumsum(onehot, axis=0) - onehot) * onehot, axis=-1)
    dest_slot = owners * send_cap + ranks
    total_slots = wide_size * send_cap
    outgoing = (
        jnp.zeros((row_size, total_slots), jnp.float32).at[:, dest_slot].set(jnp.transpose(coarse))
    )
    received = lax.all_to_all(
        outgoing.reshape(row_size, wide_size, send_cap),
        "wide",
        split_axis=1,
        concat_axis=1,
        tiled=True,
    )
    result = received.reshape(row_size, total_slots)
    return result.reshape(1, row_size, total_slots)


def solution(mesh):
    placed = (
        P("grp", "wide", None),
        P("grp", "wide", None),
        P("grp", "wide", None),
        P("grp", "wide", None),
        P("grp", "wide", None, None),
        P("grp", "wide", None),
        P(),
    )
    return jax.shard_map(
        shards, mesh=mesh, in_specs=placed, out_specs=P("grp", "wide", None), check_vma=False
    )
```

profile of v0, /device:TPU:24, one launch (start us, length us, event | category | flops | bytes accessed | tf_op | source)
XLA Modules:
  0.0 108.6 jit_solution(5460660955622273873)
XLA Ops:
  0.0 1.2 %copy.105 = bf16[1,128,1152]{1,2,0:T(8,128)(2,1)S(1)} copy(bf16[1,128,1152]{2,1,0:T(8,128)(2,1)} %param.7) | data formatting | bytes 589824 | tf_op args[0]
  1.2 0.5 copy.109
  2.2 0.6 gather_fusion
  2.8 0.7 slice_bitcast_fusion
  3.5 3.4 %collective-permute-start = (bf16[1,16,6,192]{3,2,1,0:T(8,128)(2,1)}, bf16[1,16,6,192]{3,2,1,0:T(8,128)(2,1)}, u32[]{:S(2)}, u32[]{:S(2)}) collective-permute-start(bf16[1,16,6,192]{3,2,1,0:T(8,128)(2,1)} %get-tuple-element.16), channel_id=1, source_target_pairs={{0,32},{32,64},{64,96},{96,128},{128,160},{160,192},{192,224},{224... | collective-permute-start | bytes 110600 | tf_op jit(solution)/shard_map/ppermute | solution.py:15
  6.9 4.6 %collective-permute-start.1 = (bf16[1,16,6,192]{3,2,1,0:T(8,128)(2,1)}, bf16[1,16,6,192]{3,2,1,0:T(8,128)(2,1)}, u32[]{:S(2)}, u32[]{:S(2)}) collective-permute-start(bf16[1,16,6,192]{3,2,1,0:T(8,128)(2,1)} %get-tuple-element.15), channel_id=1, source_target_pairs={{32,0},{64,32},{96,64},{128,96},{160,128},{192,160},{224,192},{256... | collective-permute-start | bytes 110600 | tf_op jit(solution)/shard_map/ppermute | solution.py:18
  11.4 1.9 %collective-permute-start.2 = (bf16[1,16,6,192]{3,2,1,0:T(8,128)(2,1)}, bf16[1,16,6,192]{3,2,1,0:T(8,128)(2,1)}, u32[]{:S(2)}, u32[]{:S(2)}) collective-permute-start(bf16[1,16,6,192]{3,2,1,0:T(8,128)(2,1)} %get-tuple-element.14), channel_id=1, source_target_pairs={{0,1},{1,2},{2,3},{3,4},{4,5},{5,6},{6,7},{7,8},{8,9},{9,10},{10,1... | collective-permute-start | bytes 110600 | tf_op jit(solution)/shard_map/ppermute | solution.py:15
  13.4 1.3 %collective-permute-start.3 = (bf16[1,16,6,192]{3,2,1,0:T(8,128)(2,1)}, bf16[1,16,6,192]{3,2,1,0:T(8,128)(2,1)}, u32[]{:S(2)}, u32[]{:S(2)}) collective-permute-start(bf16[1,16,6,192]{3,2,1,0:T(8,128)(2,1)} %get-tuple-element.13), channel_id=1, source_target_pairs={{1,0},{2,1},{3,2},{4,3},{5,4},{6,5},{7,6},{8,7},{9,8},{10,9},{11,1... | collective-permute-start | bytes 110600 | tf_op jit(solution)/shard_map/ppermute | solution.py:18
  14.6 1.0 copy.106
  15.9 1.4 %reshape.281 = f32[768,192]{1,0:T(8,128)S(1)} reshape(f32[1,128,1152]{2,1,0:T(8,128)} %copy.106) | data formatting | bytes 1179648 | tf_op jit(solution)/shard_map/convert_element_type | solution.py:49
  17.4 0.3 convolution_convert_fusion.6
  17.7 1.2 %convolution_convert_fusion.5 = bf16[768,192]{0,1:T(8,128)(2,1)} fusion(bf16[768,192]{1,0:T(8,128)(2,1)S(1)} %multiply_convert_fusion.1, bf16[192,768]{1,0:T(8,128)(2,1)S(1)} %copy-done.5), kind=kOutput, calls=%fused_computation.29 | convolution fusion | flops 56770560 | bytes 786432 | tf_op jit(solution)/shard_map/dot_general | solution.py:25
  18.9 1.0 convolution_convert_fusion.4
  19.9 1.1 %convolution_convert_fusion.3 = bf16[768,192]{0,1:T(8,128)(2,1)} fusion(bf16[768,192]{1,0:T(8,128)(2,1)S(1)} %multiply_convert_fusion.1, bf16[192,768]{1,0:T(8,128)(2,1)S(1)} %copy-done.5), kind=kOutput, calls=%fused_computation.27 | convolution fusion | flops 56770560 | bytes 786432 | tf_op jit(solution)/shard_map/dot_general | solution.py:25
  21.1 0.6 fusion.23
  21.6 0.6 fusion.38
  22.9 1.2 %copy.111 = bf16[768,192]{1,0:T(8,128)(2,1)S(1)} copy(bf16[768,192]{0,1:T(8,128)(2,1)} %convolution_convert_fusion.5) | data formatting | bytes 589824 | tf_op jit(solution)/shard_map/convert_element_type | solution.py:28
  24.6 2.1 %copy.115 = bf16[768,192]{1,0:T(8,128)(2,1)} copy(bf16[768,192]{0,1:T(8,128)(2,1)} %convolution_convert_fusion.3) | data formatting | bytes 589824 | tf_op jit(solution)/shard_map/convert_element_type | solution.py:28
  26.7 1.1 %reshape.269 = bf16[128,6,192]{2,1,0:T(8,128)(2,1)S(1)} reshape(bf16[768,192]{1,0:T(8,128)(2,1)} %copy.115) | data formatting | bytes 589824 | tf_op jit(solution)/shard_map/reshape | solution.py:28
  28.1 0.8 select_reduce_fusion
  28.9 0.7 fusion.22
  29.6 0.7 pad_clamp_fusion
  30.6 1.0 fusion.7
  32.5 0.9 bitcast_dynamic-update-slice_fusion.3
  33.3 0.8 bitcast_dynamic-update-slice_fusion.2
  34.2 0.8 bitcast_dynamic-update-slice_fusion.1
  35.0 0.8 bitcast_dynamic-update-slice_fusion
  35.9 0.6 gather_fusion.2
  36.8 0.3 convolution_convert_fusion.1
  37.4 1.1 %fusion.4 = f32[1,128,6,6]{3,2,1,0:T(8,128)} fusion(bf16[128,6,192]{2,1,0:T(8,128)(2,1)S(1)} %reshape.274, bf16[128,6,192]{2,1,0:T(8,128)(2,1)S(1)} %gather_fusion.2, f32[128]{0:T(128)S(1)} %copy-done.11), kind=kOutput, calls=%fused_computation.15 | convolution fusion | flops 1774080 | bytes 608768 | tf_op jit(solution)/shard_map/amd,and->amn/dot_general | solution.py:32
  38.5 0.6 gather_fusion.3
  39.4 0.4 convolution_convert_fusion
  40.2 1.1 %fusion.3 = f32[1,128,6,6]{3,2,1,0:T(8,128)} fusion(bf16[128,6,192]{2,1,0:T(8,128)(2,1)S(1)} %reshape.276, bf16[128,6,192]{2,1,0:T(8,128)(2,1)S(1)} %gather_fusion.3, f32[128]{0:T(128)S(1)} %get-tuple-element.24), kind=kOutput, calls=%fused_computation.13 | convolution fusion | flops 1774080 | bytes 608768 | tf_op jit(solution)/shard_map/amd,and->amn/dot_general | solution.py:32
  41.3 0.6 gather_fusion.1
  42.2 1.3 %convolution_convert_fusion.2 = bf16[768,192]{0,1:T(8,128)(2,1)S(1)} fusion(bf16[768,192]{1,0:T(8,128)(2,1)S(1)} %reshape.271, bf16[192,768]{1,0:T(8,128)(2,1)} %param.13), kind=kOutput, calls=%fused_computation.26 | convolution fusion | flops 56770560 | bytes 688128 | tf_op jit(solution)/shard_map/dot_general | solution.py:25
  44.2 1.4 %pad_maximum_fusion = f32[3,128,6,6]{3,2,1,0:T(8,128)S(1)} fusion(f32[1,128,6,6]{3,2,1,0:T(8,128)} %fusion.3, f32[1,128,6,6]{3,2,1,0:T(8,128)} %fusion.4, f32[1,128,6,6]{3,2,1,0:T(8,128)S(1)} %fusion.5), kind=kLoop, calls=%fused_computation.5 | loop fusion | flops 27648 | bytes 110592 | tf_op jit(solution)/shard_map/stack | solution.py:82
  45.6 0.5 copy.120
  46.2 0.3 fusion.9
  46.6 1.9 %collective-permute-start.4 = (f32[1,16,36]{1,2,0:T(8,128)S(1)}, f32[1,16,36]{1,2,0:T(8,128)S(1)}, u32[]{:S(2)}, u32[]{:S(2)}) collective-permute-start(f32[1,16,36]{1,2,0:T(8,128)S(1)} %get-tuple-element.17), channel_id=1, source_target_pairs={{0,32},{32,64},{64,96},{96,128},{128,160},{160,192},{192,224},{224... | collective-permute-start | bytes 6920 | tf_op jit(solution)/shard_map/ppermute | solution.py:15
  48.5 6.0 %collective-permute-start.5 = (f32[1,16,36]{1,2,0:T(8,128)S(1)}, f32[1,16,36]{1,2,0:T(8,128)S(1)}, u32[]{:S(2)}, u32[]{:S(2)}) collective-permute-start(f32[1,16,36]{1,2,0:T(8,128)S(1)} %get-tuple-element.20), channel_id=1, source_target_pairs={{32,0},{64,32},{96,64},{128,96},{160,128},{192,160},{224,192},{256... | collective-permute-start | bytes 6920 | tf_op jit(solution)/shard_map/ppermute | solution.py:18
  54.6 4.0 %collective-permute-start.6 = (f32[1,16,36]{1,2,0:T(8,128)S(1)}, f32[1,16,36]{1,2,0:T(8,128)S(1)}, u32[]{:S(2)}, u32[]{:S(2)}) collective-permute-start(f32[1,16,36]{1,2,0:T(8,128)S(1)} %get-tuple-element.19), channel_id=1, source_target_pairs={{0,1},{1,2},{2,3},{3,4},{4,5},{5,6},{6,7},{7,8},{8,9},{9,10},{10,1... | collective-permute-start | bytes 6920 | tf_op jit(solution)/shard_map/ppermute | solution.py:15
  58.6 1.5 %collective-permute-start.7 = (f32[1,16,36]{1,2,0:T(8,128)S(1)}, f32[1,16,36]{1,2,0:T(8,128)S(1)}, u32[]{:S(2)}, u32[]{:S(2)}) collective-permute-start(f32[1,16,36]{1,2,0:T(8,128)S(1)} %get-tuple-element.18), channel_id=1, source_target_pairs={{1,0},{2,1},{3,2},{4,3},{5,4},{6,5},{7,6},{8,7},{9,8},{10,9},{11,1... | collective-permute-start | bytes 6920 | tf_op jit(solution)/shard_map/ppermute | solution.py:18
  60.1 1.3 %fusion.1 = f32[128,1,6,6]{3,2,0,1:T(8,128)S(1)} fusion(bf16[128,6,192]{2,1,0:T(8,128)(2,1)} %copy-done.4, bf16[128,6,192]{2,1,0:T(8,128)(2,1)S(1)} %gather_fusion.2, f32[128]{0:T(128)S(1)} %copy-done.15), kind=kOutput, calls=%fused_computation.9 | convolution fusion | flops 1774080 | bytes 608768 | tf_op jit(solution)/shard_map/amd,and->amn/dot_general | solution.py:32
  61.6 0.3 fusion
  62.1 0.3 copy-done.1
  63.9 1.1 scatter_custom_fusion
  65.0 42.9 %all_to_all.5 = f32[144,32,8]{0,2,1:T(8,128)S(1)} all-to-all(f32[144,32,8]{0,2,1:T(8,128)S(1)} %bitcast.158), channel_id=1, replica_groups=mesh['grp'=16,'wide'=32] {'wide'}, dimensions={1} | all-to-all | bytes 294912 | tf_op jit(solution)/shard_map/all_to_all | solution.py:105
  107.9 0.8 copy.129
  (97 shorter events, 7.1 us)
Async XLA Ops:
  0.0 1.7 %copy-start.8 = (s32[1,128,64]{1,2,0:T(8,128)S(1)}, s32[1,128,64]{1,2,0:T(8,128)}, u32[]{:S(2)}) copy-start(s32[1,128,64]{1,2,0:T(8,128)} %param.8) | copy-start | bytes 98308
  1.2 0.8 copy-start.9
  3.5 29.0 %collective-permute-start = (bf16[1,16,6,192]{3,2,1,0:T(8,128)(2,1)}, bf16[1,16,6,192]{3,2,1,0:T(8,128)(2,1)}, u32[]{:S(2)}, u32[]{:S(2)}) collective-permute-start(bf16[1,16,6,192]{3,2,1,0:T(8,128)(2,1)} %get-tuple-element.16), channel_id=1, source_target_pairs={{0,32},{32,64},{64,96},{96,128},{128,160},{160,192},{192,224},{224... | collective-permute-start | bytes 110600 | tf_op jit(solution)/shard_map/ppermute | solution.py:15
  6.9 26.5 %collective-permute-start.1 = (bf16[1,16,6,192]{3,2,1,0:T(8,128)(2,1)}, bf16[1,16,6,192]{3,2,1,0:T(8,128)(2,1)}, u32[]{:S(2)}, u32[]{:S(2)}) collective-permute-start(bf16[1,16,6,192]{3,2,1,0:T(8,128)(2,1)} %get-tuple-element.15), channel_id=1, source_target_pairs={{32,0},{64,32},{96,64},{128,96},{160,128},{192,160},{224,192},{256... | collective-permute-start | bytes 110600 | tf_op jit(solution)/shard_map/ppermute | solution.py:18
  11.4 22.7 %collective-permute-start.2 = (bf16[1,16,6,192]{3,2,1,0:T(8,128)(2,1)}, bf16[1,16,6,192]{3,2,1,0:T(8,128)(2,1)}, u32[]{:S(2)}, u32[]{:S(2)}) collective-permute-start(bf16[1,16,6,192]{3,2,1,0:T(8,128)(2,1)} %get-tuple-element.14), channel_id=1, source_target_pairs={{0,1},{1,2},{2,3},{3,4},{4,5},{5,6},{6,7},{7,8},{8,9},{9,10},{10,1... | collective-permute-start | bytes 110600 | tf_op jit(solution)/shard_map/ppermute | solution.py:15
  13.4 21.7 %collective-permute-start.3 = (bf16[1,16,6,192]{3,2,1,0:T(8,128)(2,1)}, bf16[1,16,6,192]{3,2,1,0:T(8,128)(2,1)}, u32[]{:S(2)}, u32[]{:S(2)}) collective-permute-start(bf16[1,16,6,192]{3,2,1,0:T(8,128)(2,1)} %get-tuple-element.13), channel_id=1, source_target_pairs={{1,0},{2,1},{3,2},{4,3},{5,4},{6,5},{7,6},{8,7},{9,8},{10,9},{11,1... | collective-permute-start | bytes 110600 | tf_op jit(solution)/shard_map/ppermute | solution.py:18
  15.8 1.5 %copy-start.5 = (bf16[192,768]{1,0:T(8,128)(2,1)S(1)}, bf16[192,768]{1,0:T(8,128)(2,1)}, u32[]{:S(2)}) copy-start(bf16[192,768]{1,0:T(8,128)(2,1)} %param.13) | copy-start | bytes 884740
  17.4 3.7 %copy-start.10 = (s32[1,128,3]{1,0,2:T(1,128)S(1)}, s32[1,128,3]{1,0,2:T(1,128)}, u32[]{:S(2)}) copy-start(s32[1,128,3]{1,0,2:T(1,128)} %param.9) | copy-start | bytes 4612
  17.4 4.2 %copy-start.17 = (s32[1,128,3]{1,0,2:T(1,128)S(1)}, s32[1,128,3]{1,0,2:T(1,128)}, u32[]{:S(2)}) copy-start(s32[1,128,3]{1,0,2:T(1,128)} %param.10) | copy-start | bytes 4612
  22.9 1.4 %copy-start.7 = (bf16[768,192]{0,1:T(8,128)(2,1)S(1)}, bf16[768,192]{0,1:T(8,128)(2,1)}, u32[]{:S(2)}) copy-start(bf16[768,192]{0,1:T(8,128)(2,1)} %convolution_convert_fusion.4) | copy-start | bytes 884740
  24.2 6.1 %copy-start = (bf16[128,6,192]{2,1,0:T(8,128)(2,1)}, bf16[128,6,192]{2,1,0:T(8,128)(2,1)S(1)}, u32[]{:S(2)}) copy-start(bf16[128,6,192]{2,1,0:T(8,128)(2,1)S(1)} %reshape.267) | copy-start | bytes 884740
  24.2 3.6 %copy-start.12 = (s32[1,128,1]{1,2,0:T(1,128)S(1)}, s32[1,128,1]{1,2,0:T(1,128)}, u32[]{:S(2)}) copy-start(s32[1,128,1]{1,2,0:T(1,128)} %param.12) | copy-start | bytes 1540
  24.6 11.9 %copy-start.4 = (bf16[128,6,192]{2,1,0:T(8,128)(2,1)}, bf16[128,6,192]{2,1,0:T(8,128)(2,1)S(1)}, u32[]{:S(2)}) copy-start(bf16[128,6,192]{2,1,0:T(8,128)(2,1)S(1)} %reshape.268) | copy-start | bytes 884740
  27.8 3.8 %copy-start.2 = (bf16[128,6,192]{2,1,0:T(8,128)(2,1)}, bf16[128,6,192]{2,1,0:T(8,128)(2,1)S(1)}, u32[]{:S(2)}) copy-start(bf16[128,6,192]{2,1,0:T(8,128)(2,1)S(1)} %reshape.269) | copy-start | bytes 884740
  31.6 0.6 copy-start.16
  31.9 4.9 %copy-start.6 = (bf16[192,768]{1,0:T(8,128)(2,1)S(1)}, bf16[192,768]{1,0:T(8,128)(2,1)}, u32[]{:S(2)}) copy-start(bf16[192,768]{1,0:T(8,128)(2,1)} %param.13) | copy-start | bytes 884740
  36.5 0.9 copy-start.11
  45.6 14.5 %copy-start.15 = (f32[128]{0:T(128)S(1)}, f32[128]{0:T(128)}, u32[]{:S(2)}) copy-start(f32[128]{0:T(128)} %get-tuple-element.21) | copy-start | bytes 1540
  46.2 15.5 %copy-start.3 = (bf16[128,6,192]{2,1,0:T(8,128)(2,1)S(1)}, bf16[128,6,192]{2,1,0:T(8,128)(2,1)}, u32[]{:S(2)}) copy-start(bf16[128,6,192]{2,1,0:T(8,128)(2,1)} %copy-done.2) | copy-start | bytes 884740
  46.2 15.5 %copy-start.14 = (f32[128]{0:T(128)S(1)}, f32[128]{0:T(128)}, u32[]{:S(2)}) copy-start(f32[128]{0:T(128)} %get-tuple-element.23) | copy-start | bytes 1540
  46.6 16.4 %collective-permute-start.4 = (f32[1,16,36]{1,2,0:T(8,128)S(1)}, f32[1,16,36]{1,2,0:T(8,128)S(1)}, u32[]{:S(2)}, u32[]{:S(2)}) collective-permute-start(f32[1,16,36]{1,2,0:T(8,128)S(1)} %get-tuple-element.17), channel_id=1, source_target_pairs={{0,32},{32,64},{64,96},{96,128},{128,160},{160,192},{192,224},{224... | collective-permute-start | bytes 6920 | tf_op jit(solution)/shard_map/ppermute | solution.py:15
  48.5 14.6 %collective-permute-start.5 = (f32[1,16,36]{1,2,0:T(8,128)S(1)}, f32[1,16,36]{1,2,0:T(8,128)S(1)}, u32[]{:S(2)}, u32[]{:S(2)}) collective-permute-start(f32[1,16,36]{1,2,0:T(8,128)S(1)} %get-tuple-element.20), channel_id=1, source_target_pairs={{32,0},{64,32},{96,64},{128,96},{160,128},{192,160},{224,192},{256... | collective-permute-start | bytes 6920 | tf_op jit(solution)/shard_map/ppermute | solution.py:18
  54.6 8.6 %collective-permute-start.6 = (f32[1,16,36]{1,2,0:T(8,128)S(1)}, f32[1,16,36]{1,2,0:T(8,128)S(1)}, u32[]{:S(2)}, u32[]{:S(2)}) collective-permute-start(f32[1,16,36]{1,2,0:T(8,128)S(1)} %get-tuple-element.19), channel_id=1, source_target_pairs={{0,1},{1,2},{2,3},{3,4},{4,5},{5,6},{6,7},{7,8},{8,9},{9,10},{10,1... | collective-permute-start | bytes 6920 | tf_op jit(solution)/shard_map/ppermute | solution.py:15
  58.6 4.9 %collective-permute-start.7 = (f32[1,16,36]{1,2,0:T(8,128)S(1)}, f32[1,16,36]{1,2,0:T(8,128)S(1)}, u32[]{:S(2)}, u32[]{:S(2)}) collective-permute-start(f32[1,16,36]{1,2,0:T(8,128)S(1)} %get-tuple-element.18), channel_id=1, source_target_pairs={{1,0},{2,1},{3,2},{4,3},{5,4},{6,5},{7,6},{8,7},{9,8},{10,9},{11,1... | collective-permute-start | bytes 6920 | tf_op jit(solution)/shard_map/ppermute | solution.py:18
  61.4 1.0 copy-start.1
  61.4 1.0 copy-start.13
where the time goes:
time: 109 us
  blocking collectives  42.9 us (39%)
  starting transfers between devices  24.6 us (23%)
  local copies, waits for them, and re-layouts  22.4 us (21%)
  matrix products  12.5 us (11%)
  other arithmetic  5.36 us (5%)
    all_to_all x1, blocking collectives, shards(): lax.all_to_all(outgoing.reshape(row_size, wide_size, send_cap), 'wide', s...  42.9 us
    ppermute x4, starting transfers between devices, padded(): lax.ppermute(lax.slice_in_dim(block, 0, width, axis=dim), axis, backward)  13.3 us
    ppermute x4, starting transfers between devices, padded(): lax.ppermute(lax.slice_in_dim(block, block.shape[dim] - width, None, axis...  11.2 us
    dot_general x10, matrix products, paired(): jnp.einsum('amd,and->amn', left, right, preferred_element_type=jnp.float32)  6.27 us
    dot_general x7, matrix products, project(): jnp.dot(left.reshape(count * modes_count, dofs_count), matrix, preferred_...  5.7 us
    unnamed x43, local copies, waits for them, and re-layouts  4.46 us
    convert_element_type x7, local copies, waits for them, and re-layouts, project(): return product.astype(jnp.bfloat16).reshape(count, modes_count, dofs_count)  4.13 us
    convert_element_type x3, local copies, waits for them, and re-layouts, shards(): raw_modes.astype(jnp.float32) * scales[:, None, :]  2.88 us
  transfers between devices with their start and end apart: 8, of which 1 were waited for; matrix products, arithmetic and copies ran while one was open for 21% of the time, Pallas kernels for 0%

commit v1 on v0

v1 whole, which is shorter than its diff:
```python
import functools

import jax
import jax.numpy as jnp
from jax import lax
from jax.experimental import pallas as pl
from jax.experimental.pallas import tpu as pltpu
from jax.sharding import PartitionSpec as P

AGG = 128
MODES = 6
DOFS = 192
FACES = 3
LEVELS = 8
GHOST = 16
CAP = 8
WIDTH = MODES * DOFS
BLOCK = MODES * MODES
ROW = (1 + FACES) * BLOCK
MESSAGE = WIDTH + 128
MESH = pl.DeviceIdType.MESH
F32 = jnp.float32
BF16 = jnp.bfloat16


def lanes_dot(left, right):
    return lax.dot_general(left, right, (((1,), (1,)), ((), ())), preferred_element_type=F32)


def plain_dot(left, right):
    return jnp.dot(left, right, preferred_element_type=F32)


def ones_where(condition):
    return jnp.where(condition, 1.0, 0.0).astype(BF16)


def iota(shape, dim):
    return lax.broadcasted_iota(jnp.int32, shape, dim)


def pair_sums(load_left, load_right):
    def step(i, sums):
        base = pl.multiple_of(i * 16, 16)
        left = [load_left(m, base).astype(F32) for m in range(MODES)]
        right = [load_right(n, base).astype(F32) for n in range(MODES)]
        new = []
        for m in range(MODES):
            for n in range(MODES):
                product = left[m] * right[n]
                new.append(sums[m * MODES + n] + (product[:8] + product[8:]))
        return tuple(new)

    zero = jnp.zeros((8, AGG), F32)
    return lax.fori_loop(0, DOFS // 16, step, (zero,) * BLOCK)


def kernel(
    grp_size, wide_size,
    null_hbm, damage_hbm, target_hbm, face_hbm, list_hbm, owner_hbm, stiff_hbm,
    out_ref,
    null_v, damage_v, target_v, face_v, list_v, owner_v, stiff_v,
    message_out, message_in, modes_t, stiff_t, near_s, other_s, partial_s, sums_s, place_s, send_s, recv_s,
    in_sem, ghost_send, ghost_recv, row_send, row_recv,
):
    g = lax.axis_index("grp")
    w = lax.axis_index("wide")

    loads = [
        pltpu.make_async_copy(source, target, in_sem.at[k])
        for k, (source, target) in enumerate(
            [
                (list_hbm, list_v), (damage_hbm, damage_v), (null_hbm, null_v), (target_hbm, target_v),
                (face_hbm, face_v), (owner_hbm, owner_v), (stiff_hbm, stiff_v),
            ]
        )
    ]
    for load in loads:
        load.start()

    barrier = pltpu.get_barrier_semaphore()

    def greet(k, carry):
        pl.semaphore_signal(barrier, inc=1, device_id=(g, lax.rem(w + k, wide_size)), device_id_type=MESH)
        return carry

    lax.fori_loop(1, wide_size, greet, 0)
    grp_lower = lax.rem(g + grp_size - 1, grp_size)
    grp_upper = lax.rem(g + 1, grp_size)
    for neighbour in (grp_lower, grp_upper):
        pl.semaphore_signal(barrier, inc=1, device_id=(neighbour, w), device_id_type=MESH)

    loads[0].wait()
    listed = list_v[...].astype(F32)
    spread = jnp.concatenate([jnp.broadcast_to(listed[r : r + 1], (GHOST, GHOST)) for r in range(4)], axis=0)
    on_diagonal = (iota((4 * GHOST, GHOST), 0) & (GHOST - 1)) == iota((4 * GHOST, GHOST), 1)
    list_column = jnp.sum(jnp.where(on_diagonal, spread, 0.0), axis=1, keepdims=True).astype(jnp.int32)
    select = ones_where(list_column == iota((4 * GHOST, AGG), 1))

    loads[1].wait()
    levels = ((LEVELS - damage_v[...]).astype(F32) * (1.0 / LEVELS)).T.astype(BF16)
    node_of = ((iota((1, WIDTH), 1) * 43691) >> 17) & 63
    widen = ones_where(iota((64, WIDTH), 0) == node_of)
    scales = plain_dot(levels, widen)
    loads[2].wait()
    modes = (null_v[...].astype(F32) * scales).astype(BF16)
    picked = plain_dot(select, modes).astype(BF16)

    loads[3].wait()
    loads[4].wait()
    targets = jnp.concatenate([target_v[f] for f in range(FACES)], axis=1)
    levels_f = jnp.concatenate([face_v[f] for f in range(FACES)], axis=1)
    level = (LEVELS - levels_f).astype(F32) * (1.0 / LEVELS)
    weight = level * level
    chosen = ones_where(iota((AGG + 4 * GHOST, FACES * AGG), 0) == targets)
    row = iota((AGG, FACES * AGG), 0)
    face_of = iota((AGG, FACES * AGG), 1) >> 7
    weight_rows = jnp.where((row == face_of) | (row == face_of + FACES), weight, 0.0).astype(BF16)
    weight_local = lanes_dot(weight_rows[:16], chosen[:AGG])
    weight_ghost = lanes_dot(chosen[AGG:], weight_rows)
    high = weight_ghost.astype(BF16).astype(F32)
    split = jnp.where(iota((4 * GHOST, 128), 1) < FACES, high, weight_ghost - high).astype(BF16)
    for r in range(4):
        message_out[r, :, :WIDTH] = picked[r * GHOST : (r + 1) * GHOST]
        message_out[r, :, WIDTH:] = split[r * GHOST : (r + 1) * GHOST]

    pl.semaphore_wait(barrier, wide_size + 1)
    wide_lower = lax.rem(w + wide_size - 1, wide_size)
    wide_upper = lax.rem(w + 1, wide_size)
    ghost_copies = [
        pltpu.make_async_remote_copy(
            src_ref=message_out.at[r],
            dst_ref=message_in.at[r ^ 1],
            send_sem=ghost_send.at[r],
            recv_sem=ghost_recv.at[r ^ 1],
            device_id=peer,
            device_id_type=MESH,
        )
        for r, peer in enumerate([(grp_lower, w), (grp_upper, w), (g, wide_lower), (g, wide_upper)])
    ]
    for copy in ghost_copies:
        copy.start()

    modes_t[...] = modes.T
    loads[6].wait()
    stiff_t[...] = stiff_v[...].T
    for pair in range(MODES // 2):
        two = jnp.concatenate(
            [modes_t[(2 * pair + h) * DOFS : (2 * pair + h + 1) * DOFS] for h in range(2)], axis=1
        )
        product = plain_dot(stiff_t[...], two).astype(BF16)
        near_s[2 * pair] = product[:, :AGG]
        near_s[2 * pair + 1] = product[:, AGG:]

    loads[5].wait()
    owner = owner_v[0]
    owned = iota((wide_size, AGG), 0) == owner
    before = ones_where(iota((AGG, AGG), 0) < iota((AGG, AGG), 1))
    earlier = plain_dot(ones_where(owned), before)
    rank = jnp.sum(jnp.where(owned, earlier, 0.0), axis=0, keepdims=True).astype(jnp.int32)
    place_s[...] = ones_where(iota((wide_size * CAP, AGG), 0) == owner * CAP + rank)

    def load_modes(m, base):
        return modes_t[pl.ds(m * DOFS + base, 16), :]

    for k in range(1 + FACES):
        sums = pair_sums(lambda m, base, k=k: near_s[m, pl.ds(k * DOFS + base, 16), :], load_modes)
        for entry in range(BLOCK):
            partial_s[k, entry * 8 : entry * 8 + 8] = sums[entry]

    for copy in ghost_copies:
        copy.wait_recv()
    valid = [g > 0, g < grp_size - 1, w > 0, w < wide_size - 1]
    arrived = jnp.concatenate(
        [jnp.where(valid[r], message_in[r].astype(F32), 0.0) for r in range(4)], axis=0
    ).astype(BF16)
    arrived_t = arrived.T
    ghosts_t = arrived_t[:WIDTH]
    weight_back = plain_dot(arrived_t[WIDTH : WIDTH + 16], select)
    for f in range(FACES):
        at = slice(f * AGG, (f + 1) * AGG)
        other = plain_dot(modes_t[...], chosen[:AGG, at]) + plain_dot(ghosts_t, chosen[AGG:, at])
        other_s[f] = other.astype(BF16)

    total = []
    for f in range(FACES):
        total.append(
            weight[:, f * AGG : (f + 1) * AGG]
            + weight_local[f : f + 1]
            + (weight_back[f : f + 1] + weight_back[f + FACES : f + FACES + 1])
        )
    for entry in range(BLOCK):
        at = slice(entry * 8, entry * 8 + 8)
        value = partial_s[0, at]
        for f in range(FACES):
            value = value + total[f] * partial_s[f + 1, at]
        sums_s[at] = value
    for f in range(FACES):
        sums = pair_sums(
            lambda m, base, f=f: near_s[m, pl.ds((f + 1) * DOFS + base, 16), :],
            lambda n, base, f=f: other_s[f, pl.ds(n * DOFS + base, 16), :],
        )
        negative = -weight[:, f * AGG : (f + 1) * AGG]
        for entry in range(BLOCK):
            at = ((f + 1) * BLOCK + entry) * 8
            sums_s[at : at + 8] = negative * sums[entry]

    coarse_t = sums_s[pl.ds(0, ROW, stride=8), :]
    for s in range(1, 8):
        coarse_t = coarse_t + sums_s[pl.ds(s, ROW, stride=8), :]
    coarse_t = coarse_t.astype(BF16)
    tail = jnp.concatenate([coarse_t[128:], jnp.zeros((256 - ROW, AGG), BF16)], axis=0)
    first = lanes_dot(place_s[...], coarse_t[:128]).reshape(wide_size, CAP, 128)
    second = lanes_dot(place_s[...], tail).reshape(wide_size, CAP, 128)
    send_s[...] = jnp.concatenate([first, second], axis=1).astype(BF16)

    own = pltpu.make_async_copy(send_s.at[w], recv_s.at[w], row_recv)
    own.start()

    def row_copy(k):
        peer = lax.rem(w + k, wide_size)
        return pltpu.make_async_remote_copy(
            src_ref=send_s.at[peer],
            dst_ref=recv_s.at[w],
            send_sem=row_send,
            recv_sem=row_recv,
            device_id=(g, peer),
            device_id_type=MESH,
        )

    def send_rows(k, carry):
        row_copy(k).start()
        return carry

    lax.fori_loop(1, wide_size, send_rows, 0)
    for copy in ghost_copies:
        copy.wait_send()
    pltpu.make_async_copy(recv_s, recv_s, row_recv).wait()

    rows = recv_s[...].astype(F32)
    out_ref[:128, :] = rows[:, :CAP].reshape(wide_size * CAP, 128).T
    out_ref[128:, :] = rows[:, CAP:].reshape(wide_size * CAP, 128).T[: ROW - 128]
    sent = send_s.at[pl.ds(0, wide_size - 1)]
    pltpu.make_async_copy(sent, sent, row_send).wait()


def solution(mesh):
    grp_size, wide_size = mesh.shape["grp"], mesh.shape["wide"]

    def shards(null_space, node_damage, face_target, face_damage, ghost_lists, agg_owner, stiffness):
        coarse = pl.pallas_call(
            functools.partial(kernel, grp_size, wide_size),
            out_shape=jax.ShapeDtypeStruct((ROW, wide_size * CAP), F32),
            in_specs=[pl.BlockSpec(memory_space=pltpu.HBM)] * 7,
            out_specs=pl.BlockSpec(memory_space=pltpu.VMEM),
            scratch_shapes=[
                pltpu.VMEM((AGG, WIDTH), BF16),
                pltpu.VMEM((64, AGG), jnp.int32),
                pltpu.VMEM((FACES, 1, AGG), jnp.int32),
                pltpu.VMEM((FACES, 1, AGG), jnp.int32),
                pltpu.VMEM((4, GHOST), jnp.int32),
                pltpu.VMEM((1, 1, AGG), jnp.int32),
                pltpu.VMEM((DOFS, (1 + FACES) * DOFS), BF16),
                pltpu.VMEM((4, GHOST, MESSAGE), BF16),
                pltpu.VMEM((4, GHOST, MESSAGE), BF16),
                pltpu.VMEM((WIDTH, AGG), BF16),
                pltpu.VMEM(((1 + FACES) * DOFS, DOFS), BF16),
                pltpu.VMEM((MODES, (1 + FACES) * DOFS, AGG), BF16),
                pltpu.VMEM((FACES, WIDTH, AGG), BF16),
                pltpu.VMEM((1 + FACES, BLOCK * 8, AGG), F32),
                pltpu.VMEM((ROW * 8, AGG), F32),
                pltpu.VMEM((wide_size * CAP, AGG), BF16),
                pltpu.VMEM((wide_size, 16, 128), BF16),
                pltpu.VMEM((wide_size, 16, 128), BF16),
                pltpu.SemaphoreType.DMA((7,)),
                pltpu.SemaphoreType.DMA((4,)),
                pltpu.SemaphoreType.DMA((4,)),
                pltpu.SemaphoreType.DMA,
                pltpu.SemaphoreType.DMA,
            ],
            compiler_params=pltpu.CompilerParams(
                collective_id=0, has_side_effects=True, vmem_limit_bytes=32 * 1024 * 1024
            ),
            cost_estimate=pl.CostEstimate(flops=400_000_000, bytes_accessed=1_000_000, transcendentals=0),
        )(
            null_space[0],
            jnp.transpose(node_damage[0]),
            jnp.transpose(face_target, (2, 0, 1)),
            jnp.transpose(face_damage, (2, 0, 1)),
            ghost_lists[0, 0],
            jnp.transpose(agg_owner, (0, 2, 1)),
            stiffness,
        )
        return coarse[None]

    placed = (
        P("grp", "wide", None),
        P("grp", "wide", None),
        P("grp", "wide", None),
        P("grp", "wide", None),
        P("grp", "wide", None, None),
        P("grp", "wide", None),
        P(),
    )
    return jax.shard_map(
        shards, mesh=mesh, in_specs=placed, out_specs=P("grp", "wide", None), check_vma=False
    )
```

time: 109 us -> 37.3 us (0.34)
  the two profiles are of different devices: /device:TPU:24 before, /device:TPU:1 now
where the time goes in v1:
time: 37.3 us; the launch traced here: 37.1 us
  Pallas kernels  33 us (88%)
  local copies, waits for them, and re-layouts  4.06 us (11%)
    pallas_call x1, Pallas kernels, shards(): pl.pallas_call(functools.partial(kernel, grp_size, wide_size), out_shape=...  33 us
    unnamed x15, local copies, waits for them, and re-layouts  4.06 us

profile of v1, /device:TPU:1, one launch (start us, length us, event | category | flops | bytes accessed | tf_op | source)
XLA Modules:
  0.0 37.1 jit_solution(16496643068457857166)
XLA Ops:
  0.0 0.0 copy-start.5
  0.0 0.0 copy-start.6
  0.0 0.0 copy-start.3
  0.0 0.0 copy-start.4
  0.0 0.7 %copy-done.5 = s32[1,128,3]{1,0,2:T(1,128)S(1)} copy-done((s32[1,128,3]{1,0,2:T(1,128)S(1)}, s32[1,128,3]{1,0,2:T(1,128)}, u32[]{:S(2)}) %copy-start.5) | copy-done | bytes 1560
  0.7 0.0 copy-done.6
  0.7 0.0 copy-done.3
  0.7 0.0 copy-done.4
  0.7 0.0 copy-start
  0.7 1.0 %copy-done = bf16[1,128,1152]{2,1,0:T(8,128)(2,1)S(1)} copy-done((bf16[1,128,1152]{2,1,0:T(8,128)(2,1)S(1)}, bf16[1,128,1152]{2,1,0:T(8,128)(2,1)}, u32[]{:S(2)}) %copy-start) | copy-done | bytes 294936
  1.7 0.0 copy-start.1
  1.7 1.0 %copy-done.1 = bf16[192,768]{1,0:T(8,128)(2,1)S(1)} copy-done((bf16[192,768]{1,0:T(8,128)(2,1)S(1)}, bf16[192,768]{1,0:T(8,128)(2,1)}, u32[]{:S(2)}) %copy-start.1) | copy-done | bytes 294936
  2.7 0.0 copy-start.2
  2.7 0.8 %copy-done.2 = s32[1,128,64]{1,2,0:T(8,128)S(1)} copy-done((s32[1,128,64]{1,2,0:T(8,128)S(1)}, s32[1,128,64]{1,2,0:T(8,128)}, u32[]{:S(2)}) %copy-start.2) | copy-done | bytes 32792
  3.4 33.0 %shard_map.73 = f32[144,256]{1,0:T(8,128)S(1)} custom-call(bf16[128,1152]{1,0:T(8,128)(2,1)S(1)} %bitcast.10, s32[64,128]{1,0:T(8,128)S(1)} %bitcast.11, s32[3,1,128]{2,1,0:T(1,128)S(1)} %bitcast.13, s32[3,1,128]{2,1,0:T(1,128)S(1)} %bitcast.14, s32[4,16]{1,0:T(4,128)S(1)} %bitcast.12, s32[1,1,128]{2,1,0:T(1,128)S(1)} %bitcast.15, bf16[192,768]{1,0:T(8,128)(2,1)S(1)} %copy-done.1), custom_call_target="tpu_custom_call" | custom-call | flops 400000000 | bytes 1000000 | tf_op jit(solution)/shard_map/pallas_call | solution.py:251
  36.4 0.7 %copy.9 = f32[1,144,256]{2,1,0:T(8,128)} copy(f32[1,144,256]{2,1,0:T(8,128)S(1)} %bitcast.9) | data formatting | bytes 294912
Async XLA Ops:
  0.0 0.7 %copy-start.5 = (s32[1,128,3]{1,0,2:T(1,128)S(1)}, s32[1,128,3]{1,0,2:T(1,128)}, u32[]{:S(2)}) copy-start(s32[1,128,3]{1,0,2:T(1,128)} %param.10) | copy-start | bytes 4612
  0.0 0.7 %copy-start.6 = (s32[1,128,1]{1,2,0:T(1,128)S(1)}, s32[1,128,1]{1,2,0:T(1,128)}, u32[]{:S(2)}) copy-start(s32[1,128,1]{1,2,0:T(1,128)} %param.12) | copy-start | bytes 1540
  0.0 0.7 %copy-start.3 = (s32[1,1,4,16]{3,2,1,0:T(4,128)S(1)}, s32[1,1,4,16]{3,2,1,0:T(4,128)}, u32[]{:S(2)}) copy-start(s32[1,1,4,16]{3,2,1,0:T(4,128)} %param.11) | copy-start | bytes 772
  0.0 0.7 %copy-start.4 = (s32[1,128,3]{1,0,2:T(1,128)S(1)}, s32[1,128,3]{1,0,2:T(1,128)}, u32[]{:S(2)}) copy-start(s32[1,128,3]{1,0,2:T(1,128)} %param.9) | copy-start | bytes 4612
  0.7 1.0 %copy-start = (bf16[1,128,1152]{2,1,0:T(8,128)(2,1)S(1)}, bf16[1,128,1152]{2,1,0:T(8,128)(2,1)}, u32[]{:S(2)}) copy-start(bf16[1,128,1152]{2,1,0:T(8,128)(2,1)} %param.7) | copy-start | bytes 884740
  1.7 1.0 %copy-start.1 = (bf16[192,768]{1,0:T(8,128)(2,1)S(1)}, bf16[192,768]{1,0:T(8,128)(2,1)}, u32[]{:S(2)}) copy-start(bf16[192,768]{1,0:T(8,128)(2,1)} %stiff_hbm.1) | copy-start | bytes 884740
  2.7 0.8 %copy-start.2 = (s32[1,128,64]{1,2,0:T(8,128)S(1)}, s32[1,128,64]{1,2,0:T(8,128)}, u32[]{:S(2)}) copy-start(s32[1,128,64]{1,2,0:T(8,128)} %param.8) | copy-start | bytes 98308

commit v2 on v1

--- a/solution.py
+++ b/solution.py
@@ -61,10 +61,26 @@
     out_ref,
     null_v, damage_v, target_v, face_v, list_v, owner_v, stiff_v,
     message_out, message_in, modes_t, stiff_t, near_s, other_s, partial_s, sums_s, place_s, send_s, recv_s,
-    in_sem, ghost_send, ghost_recv, row_send, row_recv,
+    in_sem, ghost_send, ghost_recv, row_send, row_recv, everyone,
 ):
     g = lax.axis_index("grp")
     w = lax.axis_index("wide")
+
+    barrier = pltpu.get_barrier_semaphore()
+    neighbours = [(g - 1, w), (g + 1, w), (g, w - 1), (g, w + 1)]
+    valid = [g > 0, g < grp_size - 1, w > 0, w < wide_size - 1]
+    hubs = (wide_size // 2, wide_size - 1)
+    is_hub = (w == hubs[0]) | (w == hubs[1])
+
+    def greet(peer, condition):
+        @pl.when(condition)
+        def _():
+            pl.semaphore_signal(barrier, inc=1, device_id=peer, device_id_type=MESH)
+
+    for peer, condition in zip(neighbours, valid):
+        greet(peer, condition)
+    for hub in hubs:
+        greet((g, hub), w != hub)
 
     loads = [
         pltpu.make_async_copy(source, target, in_sem.at[k])
@@ -77,18 +93,6 @@
     ]
     for load in loads:
         load.start()
-
-    barrier = pltpu.get_barrier_semaphore()
-
-    def greet(k, carry):
-        pl.semaphore_signal(barrier, inc=1, device_id=(g, lax.rem(w + k, wide_size)), device_id_type=MESH)
-        return carry
-
-    lax.fori_loop(1, wide_size, greet, 0)
-    grp_lower = lax.rem(g + grp_size - 1, grp_size)
-    grp_upper = lax.rem(g + 1, grp_size)
-    for neighbour in (grp_lower, grp_upper):
-        pl.semaphore_signal(barrier, inc=1, device_id=(neighbour, w), device_id_type=MESH)
 
     loads[0].wait()
     listed = list_v[...].astype(F32)
@@ -124,22 +128,41 @@
         message_out[r, :, :WIDTH] = picked[r * GHOST : (r + 1) * GHOST]
         message_out[r, :, WIDTH:] = split[r * GHOST : (r + 1) * GHOST]
 
-    pl.semaphore_wait(barrier, wide_size + 1)
-    wide_lower = lax.rem(w + wide_size - 1, wide_size)
-    wide_upper = lax.rem(w + 1, wide_size)
+    for r in range(4):
+        @pl.when(jnp.logical_not(valid[r]))
+        def _(r=r):
+            message_in[r] = jnp.zeros((GHOST, MESSAGE), BF16)
+
+    near_count = sum(condition.astype(jnp.int32) for condition in valid)
+    pl.semaphore_wait(barrier, near_count + is_hub.astype(jnp.int32) * (wide_size - 1))
     ghost_copies = [
         pltpu.make_async_remote_copy(
             src_ref=message_out.at[r],
             dst_ref=message_in.at[r ^ 1],
             send_sem=ghost_send.at[r],
             recv_sem=ghost_recv.at[r ^ 1],
-            device_id=peer,
+            device_id=neighbours[r],
             device_id_type=MESH,
         )
-        for r, peer in enumerate([(grp_lower, w), (grp_upper, w), (g, wide_lower), (g, wide_upper)])
+        for r in range(4)
     ]
-    for copy in ghost_copies:
-        copy.start()
+    for r in range(4):
+        pl.when(valid[r])(ghost_copies[r].start)
+
+    @pl.when(is_hub)
+    def _():
+        first_told = jnp.where(w == hubs[0], wide_size // 4, wide_size // 4 * 3)
+
+        def tell(k, carry):
+            peer = lax.rem(first_told + k, wide_size)
+
+            @pl.when(peer != w)
+            def _():
+                pl.semaphore_signal(everyone, inc=1, device_id=(g, peer), device_id_type=MESH)
+
+            return carry
+
+        lax.fori_loop(0, wide_size // 2, tell, 0)
 
     modes_t[...] = modes.T
     loads[6].wait()
@@ -168,12 +191,9 @@
         for entry in range(BLOCK):
             partial_s[k, entry * 8 : entry * 8 + 8] = sums[entry]
 
-    for copy in ghost_copies:
-        copy.wait_recv()
-    valid = [g > 0, g < grp_size - 1, w > 0, w < wide_size - 1]
-    arrived = jnp.concatenate(
-        [jnp.where(valid[r], message_in[r].astype(F32), 0.0) for r in range(4)], axis=0
-    ).astype(BF16)
+    for r in range(4):
+        pl.when(valid[r])(ghost_copies[r ^ 1].wait_recv)
+    arrived = jnp.concatenate([message_in[r] for r in range(4)], axis=0)
     arrived_t = arrived.T
     ghosts_t = arrived_t[:WIDTH]
     weight_back = plain_dot(arrived_t[WIDTH : WIDTH + 16], select)
@@ -214,6 +234,7 @@
     second = lanes_dot(place_s[...], tail).reshape(wide_size, CAP, 128)
     send_s[...] = jnp.concatenate([first, second], axis=1).astype(BF16)
 
+    pl.when(jnp.logical_not(is_hub))(lambda: pl.semaphore_wait(everyone, 1))
     own = pltpu.make_async_copy(send_s.at[w], recv_s.at[w], row_recv)
     own.start()
 
@@ -233,8 +254,8 @@
         return carry
 
     lax.fori_loop(1, wide_size, send_rows, 0)
-    for copy in ghost_copies:
-        copy.wait_send()
+    for r in range(4):
+        pl.when(valid[r])(ghost_copies[r].wait_send)
     pltpu.make_async_copy(recv_s, recv_s, row_recv).wait()
 
     rows = recv_s[...].astype(F32)
@@ -277,9 +298,10 @@
                 pltpu.SemaphoreType.DMA((4,)),
                 pltpu.SemaphoreType.DMA,
                 pltpu.SemaphoreType.DMA,
+                pltpu.SemaphoreType.REGULAR,
             ],
             compiler_params=pltpu.CompilerParams(
-                collective_id=0, has_side_effects=True, vmem_limit_bytes=32 * 1024 * 1024
+                collective_id=0, has_side_effects=True, vmem_limit_bytes=56 * 1024 * 1024
             ),
             cost_estimate=pl.CostEstimate(flops=400_000_000, bytes_accessed=1_000_000, transcendentals=0),
         )(

time: 37.3 us -> 31.8 us (0.85)
  the two profiles are of different devices: /device:TPU:1 before, /device:TPU:24 now
where the time goes in v2:
time: 31.8 us; the launch traced here: 31.4 us
  Pallas kernels  29.8 us (94%)
  local copies, waits for them, and re-layouts  1.58 us (5%)
    pallas_call x1, Pallas kernels, shards(): pl.pallas_call(functools.partial(kernel, grp_size, wide_size), out_shape=...  29.8 us
    unnamed x1, local copies, waits for them, and re-layouts  1.58 us

profile of v2, /device:TPU:24, one launch (start us, length us, event | category | flops | bytes accessed | tf_op | source)
XLA Modules:
  0.0 31.4 jit_solution(2409838687075799811)
XLA Ops:
  0.0 29.8 %shard_map.73 = f32[144,256]{1,0:T(8,128)} custom-call(bf16[128,1152]{1,0:T(8,128)(2,1)} %bitcast.10, s32[64,128]{1,0:T(8,128)} %bitcast.11, s32[3,1,128]{2,1,0:T(1,128)} %bitcast.13, s32[3,1,128]{2,1,0:T(1,128)} %bitcast.14, s32[4,16]{1,0:T(4,128)} %bitcast.12, s32[1,1,128]{2,1,0:T(1,128)} %bitcast.15, bf16[192,768]{1,0:T(8,128)(2,1)} %stiff_hbm.1), custom_call_target="tpu_custom_call" | custom-call | flops 400000000 | bytes 1000000 | tf_op jit(solution)/shard_map/pallas_call | solution.py:272
  29.8 1.6 %copy.9 = f32[1,144,256]{2,1,0:T(8,128)} copy(f32[1,144,256]{2,1,0:T(8,128)} %bitcast.9) | data formatting | bytes 294912

commit v3 on v2

--- a/solution.py
+++ b/solution.py
@@ -55,12 +55,26 @@
     return lax.fori_loop(0, DOFS // 16, step, (zero,) * BLOCK)
 
 
+def row_sums(parts):
+    sub = iota((8, AGG), 0)
+
+    def halves(low, high, bit):
+        low = low + pltpu.roll(low, 8 - bit, 0)
+        high = high + pltpu.roll(high, bit, 0)
+        return jnp.where((sub & bit) == 0, low, high)
+
+    for bit in (4, 2, 1):
+        count = len(parts) // 2
+        parts = [halves(parts[i], parts[i + count], bit) for i in range(count)]
+    return parts[0]
+
+
 def kernel(
     grp_size, wide_size,
     null_hbm, damage_hbm, target_hbm, face_hbm, list_hbm, owner_hbm, stiff_hbm,
     out_ref,
     null_v, damage_v, target_v, face_v, list_v, owner_v, stiff_v,
-    message_out, message_in, modes_t, stiff_t, near_s, other_s, partial_s, sums_s, place_s, send_s, recv_s,
+    message_out, message_in, modes_t, stiff_t, near_s, other_s, diag_s, partial_s, place_s, send_s, recv_s,
     in_sem, ghost_send, ghost_recv, row_send, row_recv, everyone,
 ):
     g = lax.axis_index("grp")
@@ -171,36 +185,58 @@
         two = jnp.concatenate(
             [modes_t[(2 * pair + h) * DOFS : (2 * pair + h + 1) * DOFS] for h in range(2)], axis=1
         )
-        product = plain_dot(stiff_t[...], two).astype(BF16)
-        near_s[2 * pair] = product[:, :AGG]
-        near_s[2 * pair + 1] = product[:, AGG:]
+        near_s[pair] = plain_dot(stiff_t[...], two).astype(BF16)
+    for f in range(FACES):
+        other_s[f] = plain_dot(modes_t[...], chosen[:AGG, f * AGG : (f + 1) * AGG]).astype(BF16)
 
     loads[5].wait()
     owner = owner_v[0]
     owned = iota((wide_size, AGG), 0) == owner
+    owned_ones = ones_where(owned)
     before = ones_where(iota((AGG, AGG), 0) < iota((AGG, AGG), 1))
-    earlier = plain_dot(ones_where(owned), before)
+    earlier = plain_dot(owned_ones, before)
     rank = jnp.sum(jnp.where(owned, earlier, 0.0), axis=0, keepdims=True).astype(jnp.int32)
     place_s[...] = ones_where(iota((wide_size * CAP, AGG), 0) == owner * CAP + rank)
 
+    def load_near(k):
+        def load(m, base):
+            return near_s[m // 2, pl.ds(k * DOFS + base, 16), m % 2 * AGG : (m % 2 + 1) * AGG]
+
+        return load
+
     def load_modes(m, base):
         return modes_t[pl.ds(m * DOFS + base, 16), :]
 
+    zero = jnp.zeros((8, AGG), F32)
     for k in range(1 + FACES):
-        sums = pair_sums(lambda m, base, k=k: near_s[m, pl.ds(k * DOFS + base, 16), :], load_modes)
+        sums = list(pair_sums(load_near(k), load_modes)) + [zero] * 4
+        for entry in range(0, BLOCK, 8):
+            diag_s[k, entry : entry + 8] = row_sums(sums[entry : entry + 8])
+    for f in range(FACES):
+        sums = pair_sums(load_near(f + 1), lambda n, base, f=f: other_s[f, pl.ds(n * DOFS + base, 16), :])
         for entry in range(BLOCK):
-            partial_s[k, entry * 8 : entry * 8 + 8] = sums[entry]
+            partial_s[f, entry * 8 : entry * 8 + 8] = sums[entry]
 
     for r in range(4):
         pl.when(valid[r])(ghost_copies[r ^ 1].wait_recv)
     arrived = jnp.concatenate([message_in[r] for r in range(4)], axis=0)
-    arrived_t = arrived.T
-    ghosts_t = arrived_t[:WIDTH]
-    weight_back = plain_dot(arrived_t[WIDTH : WIDTH + 16], select)
-    for f in range(FACES):
-        at = slice(f * AGG, (f + 1) * AGG)
-        other = plain_dot(modes_t[...], chosen[:AGG, at]) + plain_dot(ghosts_t, chosen[AGG:, at])
-        other_s[f] = other.astype(BF16)
+    ghosts = jnp.concatenate([arrived[:, n * DOFS : (n + 1) * DOFS] for n in range(MODES)], axis=0)
+    weight_back = plain_dot(arrived[:, WIDTH:].T[:16], select)
+    parts = [zero] * 4
+    scale = []
+    for f in range(FACES):
+        target = jnp.broadcast_to(targets[:, f * AGG : (f + 1) * AGG], (8, AGG)) - AGG
+        wanted = [iota((8, AGG), 0) + 8 * group == target for group in range(4 * GHOST // 8)]
+        for pair in range(MODES // 2):
+            product = plain_dot(ghosts, near_s[pair, (f + 1) * DOFS : (f + 2) * DOFS])
+            for half in range(2):
+                for n in range(MODES):
+                    taken = zero
+                    for group, mask in enumerate(wanted):
+                        at = n * 4 * GHOST + group * 8
+                        taken = jnp.where(mask, product[at : at + 8, half * AGG : (half + 1) * AGG], taken)
+                    entry = (2 * pair + half) * MODES + n
+                    parts.append(partial_s[f, entry * 8 : entry * 8 + 8] + taken)
 
     total = []
     for f in range(FACES):
@@ -209,58 +245,55 @@
             + weight_local[f : f + 1]
             + (weight_back[f : f + 1] + weight_back[f + FACES : f + FACES + 1])
         )
-    for entry in range(BLOCK):
-        at = slice(entry * 8, entry * 8 + 8)
-        value = partial_s[0, at]
-        for f in range(FACES):
-            value = value + total[f] * partial_s[f + 1, at]
-        sums_s[at] = value
-    for f in range(FACES):
-        sums = pair_sums(
-            lambda m, base, f=f: near_s[m, pl.ds((f + 1) * DOFS + base, 16), :],
-            lambda n, base, f=f: other_s[f, pl.ds(n * DOFS + base, 16), :],
-        )
-        negative = -weight[:, f * AGG : (f + 1) * AGG]
-        for entry in range(BLOCK):
-            at = ((f + 1) * BLOCK + entry) * 8
-            sums_s[at : at + 8] = negative * sums[entry]
-
-    coarse_t = sums_s[pl.ds(0, ROW, stride=8), :]
-    for s in range(1, 8):
-        coarse_t = coarse_t + sums_s[pl.ds(s, ROW, stride=8), :]
-    coarse_t = coarse_t.astype(BF16)
-    tail = jnp.concatenate([coarse_t[128:], jnp.zeros((256 - ROW, AGG), BF16)], axis=0)
-    first = lanes_dot(place_s[...], coarse_t[:128]).reshape(wide_size, CAP, 128)
-    second = lanes_dot(place_s[...], tail).reshape(wide_size, CAP, 128)
-    send_s[...] = jnp.concatenate([first, second], axis=1).astype(BF16)
+    diag = diag_s[0]
+    for f in range(FACES):
+        diag = diag + total[f] * diag_s[f + 1]
+    faces = jnp.concatenate([row_sums(parts[e : e + 8]) for e in range(0, FACES * BLOCK + 4, 8)], axis=0)
+    factor = jnp.concatenate(
+        [jnp.zeros((4, AGG), F32)]
+        + [jnp.broadcast_to(-weight[:, f * AGG : (f + 1) * AGG], (BLOCK, AGG)) for f in range(FACES)],
+        axis=0,
+    )
+    faces = faces * factor
+    coarse_t = jnp.concatenate([diag[:32], diag[32:] + faces[:8], faces[8:]], axis=0)
+
+    first = lanes_dot(place_s[...], coarse_t[:128].astype(BF16)).astype(BF16)
+    last = jnp.concatenate([jnp.where(rank == s, coarse_t[128:], 0.0) for s in range(CAP)], axis=0).astype(BF16)
+    last = lanes_dot(owned_ones, last)
+    send_s[:, :4] = first.reshape(wide_size, 4, 2, 128)
+    send_s[:, 4] = jnp.concatenate([last[:, None], jnp.zeros((wide_size, 1, 128), F32)], axis=1).astype(BF16)
 
     pl.when(jnp.logical_not(is_hub))(lambda: pl.semaphore_wait(everyone, 1))
-    own = pltpu.make_async_copy(send_s.at[w], recv_s.at[w], row_recv)
-    own.start()
-
-    def row_copy(k):
-        peer = lax.rem(w + k, wide_size)
-        return pltpu.make_async_remote_copy(
+
+    def send_rows(i, carry):
+        k = wide_size - 2 - i
+        step = k // 2 + 1
+        peer = lax.rem(w + step + lax.rem(k, 2) * (wide_size - 2 * step), wide_size)
+        pltpu.make_async_remote_copy(
             src_ref=send_s.at[peer],
             dst_ref=recv_s.at[w],
             send_sem=row_send,
             recv_sem=row_recv,
             device_id=(g, peer),
             device_id_type=MESH,
-        )
-
-    def send_rows(k, carry):
-        row_copy(k).start()
+        ).start()
         return carry
 
-    lax.fori_loop(1, wide_size, send_rows, 0)
+    lax.fori_loop(0, wide_size - 1, send_rows, 0)
+    pltpu.make_async_copy(send_s.at[w], recv_s.at[w], row_recv).start()
     for r in range(4):
         pl.when(valid[r])(ghost_copies[r].wait_send)
+    column = iota((wide_size, wide_size * CAP), 1)
+    sender = ones_where(column // CAP == iota((wide_size, wide_size * CAP), 0))
     pltpu.make_async_copy(recv_s, recv_s, row_recv).wait()
 
-    rows = recv_s[...].astype(F32)
-    out_ref[:128, :] = rows[:, :CAP].reshape(wide_size * CAP, 128).T
-    out_ref[128:, :] = rows[:, CAP:].reshape(wide_size * CAP, 128).T[: ROW - 128]
+    out_ref[:128, :] = recv_s[:, :4].reshape(wide_size * CAP, 128).T.astype(F32)
+    last = plain_dot(recv_s[:, 4].astype(F32)[:, 0].T.astype(BF16), sender)
+    slot = lax.rem(iota((16, wide_size * CAP), 1), CAP)
+    tail = jnp.zeros((16, wide_size * CAP), F32)
+    for s in range(CAP):
+        tail = jnp.where(slot == s, last[s * 16 : (s + 1) * 16], tail)
+    out_ref[128:, :] = tail
     sent = send_s.at[pl.ds(0, wide_size - 1)]
     pltpu.make_async_copy(sent, sent, row_send).wait()
 
@@ -271,7 +304,7 @@
     def shards(null_space, node_damage, face_target, face_damage, ghost_lists, agg_owner, stiffness):
         coarse = pl.pallas_call(
             functools.partial(kernel, grp_size, wide_size),
-            out_shape=jax.ShapeDtypeStruct((ROW, wide_size * CAP), F32),
+            out_shape=pltpu.VMEM((ROW, wide_size * CAP), F32),
             in_specs=[pl.BlockSpec(memory_space=pltpu.HBM)] * 7,
             out_specs=pl.BlockSpec(memory_space=pltpu.VMEM),
             scratch_shapes=[
@@ -286,13 +319,13 @@
                 pltpu.VMEM((4, GHOST, MESSAGE), BF16),
                 pltpu.VMEM((WIDTH, AGG), BF16),
                 pltpu.VMEM(((1 + FACES) * DOFS, DOFS), BF16),
-                pltpu.VMEM((MODES, (1 + FACES) * DOFS, AGG), BF16),
+                pltpu.VMEM((MODES // 2, (1 + FACES) * DOFS, 2 * AGG), BF16),
                 pltpu.VMEM((FACES, WIDTH, AGG), BF16),
-                pltpu.VMEM((1 + FACES, BLOCK * 8, AGG), F32),
-                pltpu.VMEM((ROW * 8, AGG), F32),
+                pltpu.VMEM((1 + FACES, BLOCK + 4, AGG), F32),
+                pltpu.VMEM((FACES, BLOCK * 8, AGG), F32),
                 pltpu.VMEM((wide_size * CAP, AGG), BF16),
-                pltpu.VMEM((wide_size, 16, 128), BF16),
-                pltpu.VMEM((wide_size, 16, 128), BF16),
+                pltpu.VMEM((wide_size, 5, 2, 128), BF16),
+                pltpu.VMEM((wide_size, 5, 2, 128), BF16),
                 pltpu.SemaphoreType.DMA((7,)),
                 pltpu.SemaphoreType.DMA((4,)),
                 pltpu.SemaphoreType.DMA((4,)),

time: 31.8 us -> 27.3 us (0.86)
  Pallas kernels: 29.8 us -> 26.1 us
  local copies, waits for them, and re-layouts: 1.58 us -> 0.66 us
    pallas_call x1, Pallas kernels: 29.8 us -> 26.1 us  [shards(): pl.pallas_call(functools.partial(kernel, grp_size, wide_size), out_shape=...]
    unnamed x1, local copies, waits for them, and re-layouts: 1.58 us -> 0.66 us
where the time goes in v3:
time: 27.3 us; the launch traced here: 26.8 us
  Pallas kernels  26.1 us (96%)
  local copies, waits for them, and re-layouts  0.66 us (2%)
    pallas_call x1, Pallas kernels, shards(): pl.pallas_call(functools.partial(kernel, grp_size, wide_size), out_shape=...  26.1 us
    unnamed x1, local copies, waits for them, and re-layouts  0.66 us

profile of v3, /device:TPU:24, one launch (start us, length us, event | category | flops | bytes accessed | tf_op | source)
XLA Modules:
  0.0 26.8 jit_solution(4407871988061604922)
XLA Ops:
  0.0 26.1 %shard_map.73 = f32[144,256]{1,0:T(8,128)S(1)} custom-call(bf16[128,1152]{1,0:T(8,128)(2,1)} %bitcast.10, s32[64,128]{1,0:T(8,128)} %bitcast.11, s32[3,1,128]{2,1,0:T(1,128)} %bitcast.13, s32[3,1,128]{2,1,0:T(1,128)} %bitcast.14, s32[4,16]{1,0:T(4,128)} %bitcast.12, s32[1,1,128]{2,1,0:T(1,128)} %bitcast.15, bf16[192,768]{1,0:T(8,128)(2,1)} %stiff_hbm.1), custom_call_target="tpu_custom_call" | custom-call | flops 400000000 | bytes 1000000 | tf_op jit(solution)/shard_map/pallas_call | solution.py:305
  26.1 0.7 %copy.9 = f32[1,144,256]{2,1,0:T(8,128)} copy(f32[1,144,256]{2,1,0:T(8,128)S(1)} %bitcast.9) | data formatting | bytes 294912

commit v4 on v3

--- a/solution.py
+++ b/solution.py
@@ -52,7 +52,7 @@
         return tuple(new)
 
     zero = jnp.zeros((8, AGG), F32)
-    return lax.fori_loop(0, DOFS // 16, step, (zero,) * BLOCK)
+    return lax.fori_loop(0, DOFS // 16, step, (zero,) * BLOCK, unroll=True)
 
 
 def row_sums(parts):
@@ -83,8 +83,8 @@
     barrier = pltpu.get_barrier_semaphore()
     neighbours = [(g - 1, w), (g + 1, w), (g, w - 1), (g, w + 1)]
     valid = [g > 0, g < grp_size - 1, w > 0, w < wide_size - 1]
-    hubs = (wide_size // 2, wide_size - 1)
-    is_hub = (w == hubs[0]) | (w == hubs[1])
+    hub = wide_size * 23 // 32
+    is_hub = w == hub
 
     def greet(peer, condition):
         @pl.when(condition)
@@ -93,8 +93,7 @@
 
     for peer, condition in zip(neighbours, valid):
         greet(peer, condition)
-    for hub in hubs:
-        greet((g, hub), w != hub)
+    greet((g, hub), w != hub)
 
     loads = [
         pltpu.make_async_copy(source, target, in_sem.at[k])
@@ -163,20 +162,18 @@
     for r in range(4):
         pl.when(valid[r])(ghost_copies[r].start)
 
+    def partner(i):
+        k = wide_size - 2 - i
+        step = k // 2 + 1
+        return lax.rem(w + step + lax.rem(k, 2) * (wide_size - 2 * step), wide_size)
+
     @pl.when(is_hub)
     def _():
-        first_told = jnp.where(w == hubs[0], wide_size // 4, wide_size // 4 * 3)
-
-        def tell(k, carry):
-            peer = lax.rem(first_told + k, wide_size)
-
-            @pl.when(peer != w)
-            def _():
-                pl.semaphore_signal(everyone, inc=1, device_id=(g, peer), device_id_type=MESH)
-
+        def tell(i, carry):
+            pl.semaphore_signal(everyone, inc=1, device_id=(g, partner(i)), device_id_type=MESH)
             return carry
 
-        lax.fori_loop(0, wide_size // 2, tell, 0)
+        lax.fori_loop(0, wide_size - 1, tell, 0)
 
     modes_t[...] = modes.T
     loads[6].wait()
@@ -266,9 +263,7 @@
     pl.when(jnp.logical_not(is_hub))(lambda: pl.semaphore_wait(everyone, 1))
 
     def send_rows(i, carry):
-        k = wide_size - 2 - i
-        step = k // 2 + 1
-        peer = lax.rem(w + step + lax.rem(k, 2) * (wide_size - 2 * step), wide_size)
+        peer = partner(i)
         pltpu.make_async_remote_copy(
             src_ref=send_s.at[peer],
             dst_ref=recv_s.at[w],

time: 27.3 us -> 25.3 us (0.927)
  Pallas kernels: 26.1 us -> 24.4 us
    pallas_call x1, Pallas kernels: 26.1 us -> 24.4 us  [shards(): pl.pallas_call(functools.partial(kernel, grp_size, wide_size), out_shape=...]
where the time goes in v4:
time: 25.3 us; the launch traced here: 25 us
  Pallas kernels  24.4 us (96%)
  local copies, waits for them, and re-layouts  0.66 us (3%)
    pallas_call x1, Pallas kernels, shards(): pl.pallas_call(functools.partial(kernel, grp_size, wide_size), out_shape=...  24.4 us
    unnamed x1, local copies, waits for them, and re-layouts  0.66 us

profile of v4, /device:TPU:24, one launch (start us, length us, event | category | flops | bytes accessed | tf_op | source)
XLA Modules:
  0.0 25.0 jit_solution(4243693424746345362)
XLA Ops:
  0.0 24.4 %shard_map.73 = f32[144,256]{1,0:T(8,128)S(1)} custom-call(bf16[128,1152]{1,0:T(8,128)(2,1)} %bitcast.10, s32[64,128]{1,0:T(8,128)} %bitcast.11, s32[3,1,128]{2,1,0:T(1,128)} %bitcast.13, s32[3,1,128]{2,1,0:T(1,128)} %bitcast.14, s32[4,16]{1,0:T(4,128)} %bitcast.12, s32[1,1,128]{2,1,0:T(1,128)} %bitcast.15, bf16[192,768]{1,0:T(8,128)(2,1)} %stiff_hbm.1), custom_call_target="tpu_custom_call" | custom-call | flops 400000000 | bytes 1000000 | tf_op jit(solution)/shard_map/pallas_call | solution.py:300
  24.4 0.7 %copy.9 = f32[1,144,256]{2,1,0:T(8,128)} copy(f32[1,144,256]{2,1,0:T(8,128)S(1)} %bitcast.9) | data formatting | bytes 294912

commit v5 on v4

--- a/solution.py
+++ b/solution.py
@@ -162,15 +162,12 @@
     for r in range(4):
         pl.when(valid[r])(ghost_copies[r].start)
 
-    def partner(i):
-        k = wide_size - 2 - i
-        step = k // 2 + 1
-        return lax.rem(w + step + lax.rem(k, 2) * (wide_size - 2 * step), wide_size)
-
     @pl.when(is_hub)
     def _():
         def tell(i, carry):
-            pl.semaphore_signal(everyone, inc=1, device_id=(g, partner(i)), device_id_type=MESH)
+            step = i // 2 + 1
+            peer = lax.rem(w + step + lax.rem(i, 2) * (wide_size - 2 * step), wide_size)
+            pl.semaphore_signal(everyone, inc=1, device_id=(g, peer), device_id_type=MESH)
             return carry
 
         lax.fori_loop(0, wide_size - 1, tell, 0)
@@ -263,32 +260,37 @@
     pl.when(jnp.logical_not(is_hub))(lambda: pl.semaphore_wait(everyone, 1))
 
     def send_rows(i, carry):
-        peer = partner(i)
+        place = i + (i >= w + 1 - 2 * lax.rem(w, 2)).astype(jnp.int32)
+        peer = place + 1 - 2 * lax.rem(place, 2)
         pltpu.make_async_remote_copy(
             src_ref=send_s.at[peer],
             dst_ref=recv_s.at[w],
             send_sem=row_send,
-            recv_sem=row_recv,
+            recv_sem=row_recv.at[w // (wide_size // 2)],
             device_id=(g, peer),
             device_id_type=MESH,
         ).start()
         return carry
 
     lax.fori_loop(0, wide_size - 1, send_rows, 0)
-    pltpu.make_async_copy(send_s.at[w], recv_s.at[w], row_recv).start()
+    half = wide_size // 2
+    pltpu.make_async_copy(send_s.at[w], recv_s.at[w], row_recv.at[w // half]).start()
     for r in range(4):
         pl.when(valid[r])(ghost_copies[r].wait_send)
-    column = iota((wide_size, wide_size * CAP), 1)
-    sender = ones_where(column // CAP == iota((wide_size, wide_size * CAP), 0))
-    pltpu.make_async_copy(recv_s, recv_s, row_recv).wait()
-
-    out_ref[:128, :] = recv_s[:, :4].reshape(wide_size * CAP, 128).T.astype(F32)
-    last = plain_dot(recv_s[:, 4].astype(F32)[:, 0].T.astype(BF16), sender)
-    slot = lax.rem(iota((16, wide_size * CAP), 1), CAP)
-    tail = jnp.zeros((16, wide_size * CAP), F32)
-    for s in range(CAP):
-        tail = jnp.where(slot == s, last[s * 16 : (s + 1) * 16], tail)
-    out_ref[128:, :] = tail
+    columns = half * CAP
+    column = iota((half, columns), 1)
+    sender = ones_where(column // CAP == iota((half, columns), 0))
+    slot = lax.rem(iota((16, columns), 1), CAP)
+    for part in range(2):
+        rows = recv_s.at[pl.ds(part * half, half)]
+        at = slice(part * columns, (part + 1) * columns)
+        pltpu.make_async_copy(rows, rows, row_recv.at[part]).wait()
+        out_ref[:128, at] = rows[:, :4].reshape(columns, 128).T.astype(F32)
+        last = plain_dot(rows[:, 4].astype(F32)[:, 0].T.astype(BF16), sender)
+        tail = jnp.zeros((16, columns), F32)
+        for s in range(CAP):
+            tail = jnp.where(slot == s, last[s * 16 : (s + 1) * 16], tail)
+        out_ref[128:, at] = tail
     sent = send_s.at[pl.ds(0, wide_size - 1)]
     pltpu.make_async_copy(sent, sent, row_send).wait()
 
@@ -325,7 +327,7 @@
                 pltpu.SemaphoreType.DMA((4,)),
                 pltpu.SemaphoreType.DMA((4,)),
                 pltpu.SemaphoreType.DMA,
-                pltpu.SemaphoreType.DMA,
+                pltpu.SemaphoreType.DMA((2,)),
                 pltpu.SemaphoreType.REGULAR,
             ],
             compiler_params=pltpu.CompilerParams(

time: 25.3 us -> 25.1 us (level)
  no operation moved by 1% of the time
where the time goes in v5:
time: 25.1 us; the launch traced here: 25 us
  Pallas kernels  24.3 us (97%)
  local copies, waits for them, and re-layouts  0.66 us (3%)
    pallas_call x1, Pallas kernels, shards(): pl.pallas_call(functools.partial(kernel, grp_size, wide_size), out_shape=...  24.3 us
    unnamed x1, local copies, waits for them, and re-layouts  0.66 us

profile of v5, /device:TPU:24, one launch (start us, length us, event | category | flops | bytes accessed | tf_op | source)
XLA Modules:
  0.0 25.0 jit_solution(6135479030475937408)
XLA Ops:
  0.0 24.3 %shard_map.73 = f32[144,256]{1,0:T(8,128)S(1)} custom-call(bf16[128,1152]{1,0:T(8,128)(2,1)} %bitcast.10, s32[64,128]{1,0:T(8,128)} %bitcast.11, s32[3,1,128]{2,1,0:T(1,128)} %bitcast.13, s32[3,1,128]{2,1,0:T(1,128)} %bitcast.14, s32[4,16]{1,0:T(4,128)} %bitcast.12, s32[1,1,128]{2,1,0:T(1,128)} %bitcast.15, bf16[192,768]{1,0:T(8,128)(2,1)} %stiff_hbm.1), custom_call_target="tpu_custom_call" | custom-call | flops 400000000 | bytes 1000000 | tf_op jit(solution)/shard_map/pallas_call | solution.py:302
  24.3 0.7 %copy.9 = f32[1,144,256]{2,1,0:T(8,128)} copy(f32[1,144,256]{2,1,0:T(8,128)S(1)} %bitcast.9) | data formatting | bytes 294912

commit v6 on v5

--- a/solution.py
+++ b/solution.py
@@ -83,7 +83,7 @@
     barrier = pltpu.get_barrier_semaphore()
     neighbours = [(g - 1, w), (g + 1, w), (g, w - 1), (g, w + 1)]
     valid = [g > 0, g < grp_size - 1, w > 0, w < wide_size - 1]
-    hub = wide_size * 23 // 32
+    hub = wide_size * 21 // 32
     is_hub = w == hub
 
     def greet(peer, condition):
@@ -159,7 +159,7 @@
         )
         for r in range(4)
     ]
-    for r in range(4):
+    for r in (2, 3, 1, 0):
         pl.when(valid[r])(ghost_copies[r].start)
 
     @pl.when(is_hub)

time: 25.1 us -> 25 us (level)
  no operation moved by 1% of the time
where the time goes in v6:
time: 25 us; the launch traced here: 24.9 us
  Pallas kernels  24.2 us (97%)
  local copies, waits for them, and re-layouts  0.66 us (3%)
    pallas_call x1, Pallas kernels, shards(): pl.pallas_call(functools.partial(kernel, grp_size, wide_size), out_shape=...  24.2 us
    unnamed x1, local copies, waits for them, and re-layouts  0.66 us

profile of v6, /device:TPU:24, one launch (start us, length us, event | category | flops | bytes accessed | tf_op | source)
XLA Modules:
  0.0 24.9 jit_solution(12285163508425446739)
XLA Ops:
  0.0 24.2 %shard_map.73 = f32[144,256]{1,0:T(8,128)S(1)} custom-call(bf16[128,1152]{1,0:T(8,128)(2,1)} %bitcast.10, s32[64,128]{1,0:T(8,128)} %bitcast.11, s32[3,1,128]{2,1,0:T(1,128)} %bitcast.13, s32[3,1,128]{2,1,0:T(1,128)} %bitcast.14, s32[4,16]{1,0:T(4,128)} %bitcast.12, s32[1,1,128]{2,1,0:T(1,128)} %bitcast.15, bf16[192,768]{1,0:T(8,128)(2,1)} %stiff_hbm.1), custom_call_target="tpu_custom_call" | custom-call | flops 400000000 | bytes 1000000 | tf_op jit(solution)/shard_map/pallas_call | solution.py:302
  24.2 0.7 %copy.9 = f32[1,144,256]{2,1,0:T(8,128)} copy(f32[1,144,256]{2,1,0:T(8,128)S(1)} %bitcast.9) | data formatting | bytes 294912

commit v7 on v5

--- a/solution.py
+++ b/solution.py
@@ -251,10 +251,16 @@
     faces = faces * factor
     coarse_t = jnp.concatenate([diag[:32], diag[32:] + faces[:8], faces[8:]], axis=0)
 
-    first = lanes_dot(place_s[...], coarse_t[:128].astype(BF16)).astype(BF16)
+    main = coarse_t[:128].astype(BF16)
+    early = wide_size // 4
+
+    def main_rows(start, stop):
+        first = lanes_dot(place_s[start * CAP : stop * CAP], main).astype(BF16)
+        send_s[start:stop, :4] = first.reshape(stop - start, 4, 2, 128)
+
     last = jnp.concatenate([jnp.where(rank == s, coarse_t[128:], 0.0) for s in range(CAP)], axis=0).astype(BF16)
     last = lanes_dot(owned_ones, last)
-    send_s[:, :4] = first.reshape(wide_size, 4, 2, 128)
+    main_rows(0, early)
     send_s[:, 4] = jnp.concatenate([last[:, None], jnp.zeros((wide_size, 1, 128), F32)], axis=1).astype(BF16)
 
     pl.when(jnp.logical_not(is_hub))(lambda: pl.semaphore_wait(everyone, 1))
@@ -272,7 +278,9 @@
         ).start()
         return carry
 
-    lax.fori_loop(0, wide_size - 1, send_rows, 0)
+    lax.fori_loop(0, early - 1, send_rows, 0)
+    main_rows(early, wide_size)
+    lax.fori_loop(early - 1, wide_size - 1, send_rows, 0)
     half = wide_size // 2
     pltpu.make_async_copy(send_s.at[w], recv_s.at[w], row_recv.at[w // half]).start()
     for r in range(4):

time: 25.1 us -> 25.4 us (1.012)
  Pallas kernels: 24.3 us -> 24.6 us
    pallas_call x1, Pallas kernels: 24.3 us -> 24.6 us  [shards(): pl.pallas_call(functools.partial(kernel, grp_size, wide_size), out_shape=...]
where the time goes in v7:
time: 25.4 us; the launch traced here: 25.2 us
  Pallas kernels  24.6 us (97%)
  local copies, waits for them, and re-layouts  0.66 us (3%)
    pallas_call x1, Pallas kernels, shards(): pl.pallas_call(functools.partial(kernel, grp_size, wide_size), out_shape=...  24.6 us
    unnamed x1, local copies, waits for them, and re-layouts  0.66 us

profile of v7, /device:TPU:24, one launch (start us, length us, event | category | flops | bytes accessed | tf_op | source)
XLA Modules:
  0.0 25.2 jit_solution(9273347293282935098)
XLA Ops:
  0.0 24.6 %shard_map.73 = f32[144,256]{1,0:T(8,128)S(1)} custom-call(bf16[128,1152]{1,0:T(8,128)(2,1)} %bitcast.10, s32[64,128]{1,0:T(8,128)} %bitcast.11, s32[3,1,128]{2,1,0:T(1,128)} %bitcast.13, s32[3,1,128]{2,1,0:T(1,128)} %bitcast.14, s32[4,16]{1,0:T(4,128)} %bitcast.12, s32[1,1,128]{2,1,0:T(1,128)} %bitcast.15, bf16[192,768]{1,0:T(8,128)(2,1)} %stiff_hbm.1), custom_call_target="tpu_custom_call" | custom-call | flops 400000000 | bytes 1000000 | tf_op jit(solution)/shard_map/pallas_call | solution.py:310
  24.6 0.7 %copy.9 = f32[1,144,256]{2,1,0:T(8,128)} copy(f32[1,144,256]{2,1,0:T(8,128)S(1)} %bitcast.9) | data formatting | bytes 294912
